TPU v7x, 32 devices: a whole 2x2x4 slice. The times are simulated.
32 devices in a mesh: dp: 16 (over z, y, x), tensor: 2 (over core).
Axes of the slice: x: 2, y: 2, z: 4, core: 2. Of those that a mesh axis runs over, the one named last changes fastest.
Arguments:
- tokens: bfloat16 [32768, 768], P(('dp', 'tensor')), may hold values from -6 to 6
- out_cot: bfloat16 [32768, 768], P(('dp', 'tensor')), may hold values from -6 to 6
- norm_gain: bfloat16 [2, 768], replicated, may hold values from 0.5 to 1.5
- norm_bias: bfloat16 [2, 768], replicated, may hold values from -1.25 to 1.25
- qkv_weight: bfloat16 [3, 768, 768], P(None, None, 'tensor'), may hold values from -0.21875 to 0.21875
- qkv_bias: bfloat16 [3, 768], P(None, 'tensor'), may hold values from -1.25 to 1.25
- out_weight: bfloat16 [768, 768], P('tensor'), may hold values from -1.75 to 1.75
- out_bias: bfloat16 [2, 768], replicated, may hold values from -1.25 to 1.25
- up_weight: bfloat16 [768, 3072], P(None, 'tensor'), may hold values from -0.21875 to 0.21875
- up_bias: bfloat16 [3072], P('tensor'), may hold values from -1.25 to 1.25
- down_weight: bfloat16 [3072, 768], P('tensor'), may hold values from -0.109375 to 0.109375
- seq_lengths: int32 [64], replicated, may hold values from 1 to 1024, as said below
- seq_owner: int32 [64], replicated, may hold values from 0 to 15, as said below
Outputs:
- mixed: bfloat16 [32768, 768], P(('dp', 'tensor'))
- tokens_grad: bfloat16 [32768, 768], P(('dp', 'tensor'))
- norm_gain_grad: float32 [2, 768], replicated
- norm_bias_grad: float32 [2, 768], replicated
- qkv_weight_grad: float32 [3, 768, 768], P(None, None, 'tensor')
- qkv_bias_grad: float32 [3, 768], P(None, 'tensor')
- out_weight_grad: float32 [768, 768], P('tensor')
- out_bias_grad: float32 [2, 768], replicated
- up_weight_grad: float32 [768, 3072], P(None, 'tensor')
- up_bias_grad: float32 [3072], P('tensor')
- down_weight_grad: float32 [3072, 768], P('tensor')
Inputs may be any that keep to these rules, and one draw needn't show every extreme that they name: `seq_lengths`: each entry is the length of one sequence; at least one equals 1024. `seq_owner`: each data index holds exactly 4 sequences, laid out in list order from its slot 0; their lengths sum to at most 2048, exactly 2048 on at least one index; on every index the first sequence ends before slot 1024 and the second reaches past it.
All inputs are finite; a program needn't handle non-finite values.
Results may differ from a plain program's by a relative error of at most 0.01.
Values may be sent and summed in bfloat16 or wider, within the bound.
A program may use at most 256 MiB of HBM per device.

v0:
```python
import math

import jax
import jax.numpy as jnp
from jax import lax
from jax.sharding import PartitionSpec as P

HD = 64
ROT = 16
MAXLEN = 1024


def standard(values):
    center = values - jnp.mean(values, -1, keepdims=True)
    spread = jnp.mean(center * center, -1, keepdims=True)
    inverse = lax.rsqrt(spread + 1e-05)
    return (center * inverse, inverse)


def layout(lengths, owners, index, slot_count):
    mine = owners == index
    sizes = jnp.where(mine, lengths, 0)
    starts = jnp.cumsum(sizes) - sizes
    rows = jnp.arange(slot_count, dtype=jnp.int32)
    covers = mine[None, :] & (starts[None, :] <= rows[:, None])
    counter = jnp.sum(covers.astype(jnp.int32), 1)
    begins = jnp.max(jnp.where(covers, starts[None, :], 0), 1)
    filled = rows < jnp.sum(sizes)
    segment = jnp.where(filled, counter, lengths.shape[0] + 1 + rows)
    places = jnp.where(filled, rows - begins, 0)
    return (segment, places, filled)


def rotary(values, places):
    half = ROT // 2
    freq = 10000.0 ** (-jnp.arange(half, dtype=jnp.float32) * 2.0 / ROT)
    angles = places.astype(jnp.float32)[:, None] * freq[None, :]
    angles = jnp.concatenate([angles, angles], 1)
    cosine = jnp.cos(angles)[:, None, :]
    sine = jnp.sin(angles)[:, None, :]
    turned = values[..., :ROT]
    swapped = jnp.concatenate([-turned[..., half:], turned[..., :half]], -1)
    return jnp.concatenate([turned * cosine + swapped * sine, values[..., ROT:]], -1)


def gelu_exact(values):
    return jax.nn.gelu(values, approximate=False)


def shards(
    tokens,
    out_cot,
    norm_gain,
    norm_bias,
    qkv_weight,
    qkv_bias,
    out_weight,
    out_bias,
    up_weight,
    up_bias,
    down_weight,
    seq_lengths,
    seq_owner,
):
    rows_local = tokens.shape[0]
    slots = rows_local * lax.axis_size("tensor")
    half_index = lax.axis_index("tensor")
    segment, places, filled = layout(seq_lengths, seq_owner, lax.axis_index("dp"), slots)
    valid_local = lax.dynamic_slice_in_dim(filled, half_index * rows_local, rows_local, 0)
    scale = 1.0 / math.sqrt(HD)
    gains = norm_gain.astype(jnp.float32)
    shifts = norm_bias.astype(jnp.float32)
    x = tokens.astype(jnp.float32)
    whole_rows = lax.all_gather(tokens, "tensor", axis=0, tiled=True)
    unit_rows, inverse_rows = standard(whole_rows.astype(jnp.float32))
    first = (unit_rows * gains[0] + shifts[0]).astype(jnp.bfloat16)
    second = (unit_rows * gains[1] + shifts[1]).astype(jnp.bfloat16)
    projected = (
        jnp.einsum("sd,cde->cse", first, qkv_weight, preferred_element_type=jnp.float32)
        + qkv_bias.astype(jnp.float32)[:, None, :]
    )
    width_local = projected.shape[2]
    head_count = width_local // HD
    split = projected.reshape(3, slots, head_count, HD)

    def turn_both(query_in, key_in):
        return (rotary(query_in, places), rotary(key_in, places))

    (query_turned, key_turned), turn_pull = jax.vjp(turn_both, split[0], split[1])
    query = query_turned.astype(jnp.bfloat16)
    block_rows = min(512, MAXLEN)
    window = MAXLEN + block_rows
    front = jnp.zeros((MAXLEN, head_count, HD), jnp.bfloat16)
    key_pad = jnp.concatenate([front, key_turned.astype(jnp.bfloat16)], 0)
    value_pad = jnp.concatenate([front, split[2].astype(jnp.bfloat16)], 0)
    segment_pad = jnp.concatenate([jnp.full((MAXLEN,), -1, jnp.int32), segment], 0)

    def scored(offset):
        allowed = (
            segment[offset : offset + block_rows][:, None]
            == segment_pad[offset : offset + window][None, :]
        )
        allowed = allowed & (
            jnp.arange(window)[None, :] - MAXLEN <= jnp.arange(block_rows)[:, None]
        )
        product = (
            jnp.einsum(
                "qhd,khd->hqk",
                query[offset : offset + block_rows],
                key_pad[offset : offset + window],
                preferred_element_type=jnp.float32,
            )
            * scale
        )
        return jnp.where(allowed[None], product, -1e30)

    pieces = []
    logsums = []
    for offset in range(0, slots, block_rows):
        scores = scored(offset)
        highest = jnp.max(scores, -1, keepdims=True)
        expanded = jnp.exp(scores - highest)
        totals = jnp.sum(expanded, -1, keepdims=True)
        probs = (expanded / totals).astype(jnp.bfloat16)
        pieces.append(
            jnp.einsum(
                "hqk,khd->qhd",
                probs,
                value_pad[offset : offset + window],
                preferred_element_type=jnp.float32,
            )
        )
        logsums.append(highest + jnp.log(totals))
    attended = jnp.concatenate(pieces, 0).astype(jnp.bfloat16).reshape(slots, width_local)
    hidden = jnp.dot(second, up_weight, preferred_element_type=jnp.float32) + up_bias.astype(
        jnp.float32
    )
    active, gelu_pull = jax.vjp(gelu_exact, hidden)
    active_low = active.astype(jnp.bfloat16)
    partial_value = jnp.dot(attended, out_weight, preferred_element_type=jnp.float32) + jnp.dot(
        active_low, down_weight, preferred_element_type=jnp.float32
    )
    summed = lax.psum_scatter(
        partial_value.astype(jnp.bfloat16), "tensor", scatter_dimension=0, tiled=True
    ).astype(jnp.float32)
    biases = out_bias.astype(jnp.float32)
    mixed = (x + summed + biases[0] + biases[1]).astype(jnp.bfloat16)
    cot_local = out_cot * valid_local[:, None].astype(jnp.bfloat16)
    cot = lax.all_gather(cot_local, "tensor", axis=0, tiled=True)
    down_grad = jnp.einsum("sf,sd->fd", active_low, cot, preferred_element_type=jnp.float32)
    active_back = jnp.einsum("sd,fd->sf", cot, down_weight, preferred_element_type=jnp.float32)
    up_delta = gelu_pull(active_back)[0].astype(jnp.bfloat16)
    up_grad = jnp.einsum("sd,sf->df", second, up_delta, preferred_element_type=jnp.float32)
    up_bias_grad = jnp.sum(up_delta.astype(jnp.float32), 0)
    second_back = jnp.einsum("sf,df->sd", up_delta, up_weight, preferred_element_type=jnp.float32)
    out_w_grad = jnp.einsum("se,sd->ed", attended, cot, preferred_element_type=jnp.float32)
    attended_back = jnp.einsum("sd,ed->se", cot, out_weight, preferred_element_type=jnp.float32)
    attended_back = attended_back.astype(jnp.bfloat16).reshape(slots, head_count, HD)
    query_grads = []
    key_grad = jnp.zeros((MAXLEN + slots, head_count, HD), jnp.float32)
    value_grad = jnp.zeros((MAXLEN + slots, head_count, HD), jnp.float32)
    for number, offset in enumerate(range(0, slots, block_rows)):
        scores = scored(offset)
        probs = jnp.exp(scores - logsums[number])
        rows_back = attended_back[offset : offset + block_rows]
        prob_back = jnp.einsum(
            "qhd,khd->hqk",
            rows_back,
            value_pad[offset : offset + window],
            preferred_element_type=jnp.float32,
        )
        inner = jnp.sum(probs * prob_back, -1, keepdims=True)
        score_back = (probs * (prob_back - inner)).astype(jnp.bfloat16)
        query_grads.append(
            jnp.einsum(
                "hqk,khd->qhd",
                score_back,
                key_pad[offset : offset + window],
                preferred_element_type=jnp.float32,
            )
            * scale
        )
        key_grad = key_grad.at[offset : offset + window].add(
            jnp.einsum(
                "hqk,qhd->khd",
                score_back,
                query[offset : offset + block_rows],
                preferred_element_type=jnp.float32,
            )
            * scale
        )
        value_grad = value_grad.at[offset : offset + window].add(
            jnp.einsum(
                "hqk,qhd->khd",
                probs.astype(jnp.bfloat16),
                rows_back,
                preferred_element_type=jnp.float32,
            )
        )
    query_pre, key_pre = turn_pull((jnp.concatenate(query_grads, 0), key_grad[MAXLEN:]))
    qkv_delta = (
        jnp.stack([query_pre, key_pre, value_grad[MAXLEN:]], 0)
        .reshape(3, slots, width_local)
        .astype(jnp.bfloat16)
    )
    qkv_grad = jnp.einsum("sd,cse->cde", first, qkv_delta, preferred_element_type=jnp.float32)
    qkv_bias_grad = jnp.sum(qkv_delta.astype(jnp.float32), 1)
    first_back = jnp.einsum(
        "cse,cde->sd", qkv_delta, qkv_weight, preferred_element_type=jnp.float32
    )
    gain_grad = jnp.stack(
        [jnp.sum(first_back * unit_rows, 0), jnp.sum(second_back * unit_rows, 0)], 0
    )
    shift_grad = jnp.stack([jnp.sum(first_back, 0), jnp.sum(second_back, 0)], 0)
    combined = gains[0] * first_back + gains[1] * second_back
    combined_sum = lax.psum_scatter(
        combined.astype(jnp.bfloat16), "tensor", scatter_dimension=0, tiled=True
    ).astype(jnp.float32)
    unit_local = lax.dynamic_slice_in_dim(unit_rows, half_index * rows_local, rows_local, 0)
    inverse_local = lax.dynamic_slice_in_dim(inverse_rows, half_index * rows_local, rows_local, 0)
    average = jnp.mean(combined_sum, -1, keepdims=True)
    along = jnp.mean(combined_sum * unit_local, -1, keepdims=True)
    x_back = inverse_local * (combined_sum - average - unit_local * along)
    tokens_grad = (cot_local.astype(jnp.float32) + x_back).astype(jnp.bfloat16)
    bias_grad = jnp.sum(cot_local.astype(jnp.float32), 0)
    qkv_grad, qkv_bias_grad, out_w_grad, up_grad, up_bias_grad, down_grad = lax.psum(
        (qkv_grad, qkv_bias_grad, out_w_grad, up_grad, up_bias_grad, down_grad), "dp"
    )
    gain_grad, shift_grad, bias_grad = lax.psum(
        (gain_grad, shift_grad, bias_grad), ("dp", "tensor")
    )
    return (
        mixed,
        tokens_grad,
        gain_grad,
        shift_grad,
        qkv_grad,
        qkv_bias_grad,
        out_w_grad,
        jnp.stack([bias_grad, bias_grad], 0),
        up_grad,
        up_bias_grad,
        down_grad,
    )


def solution(mesh):
    return jax.shard_map(
        shards,
        mesh=mesh,
        in_specs=(
            P(("dp", "tensor"), None),
            P(("dp", "tensor"), None),
            P(),
            P(),
            P(None, None, "tensor"),
            P(None, "tensor"),
            P("tensor", None),
            P(),
            P(None, "tensor"),
            P("tensor"),
            P("tensor", None),
            P(),
            P(),
        ),
        out_specs=(
            P(("dp", "tensor"), None),
            P(("dp", "tensor"), None),
            P(),
            P(),
            P(None, None, "tensor"),
            P(None, "tensor"),
            P("tensor", None),
            P(),
            P(None, "tensor"),
            P("tensor"),
            P("tensor", None),
        ),
        check_vma=False,
    )
```

profile of v0, /device:TPU:0, one launch (start us, length us, event | category | flops | bytes accessed | tf_op | source)
XLA Modules:
  0.0 879.7 jit_solution(11022512712525065755)
XLA Ops:
  37.8 8.4 fusion.147
  46.3 9.6 %fusion.1 = f32[6,512]{1,0:T(8,128)} fusion(f32[6,512,1536]{2,1,0:T(8,128)} %get-tuple-element.218, f32[6,512]{1,0:T(8,128)S(1)} %get-tuple-element.217), kind=kLoop, calls=%fused_computation.26 | loop fusion | flops 9434112 | bytes 18898944 | tf_op jit(solution)/shard_map/reduce_sum | solution.py:123
  57.2 9.4 %fusion.91 = bf16[6,64,512]{2,1,0:T(8,128)(2,1)} fusion(f32[6,512,1536]{2,1,0:T(8,128)} %get-tuple-element.218, f32[6,512]{1,0:T(8,128)} %fusion.1, f32[6,512]{1,0:T(8,128)S(1)} %get-tuple-element.217, bf16[2048,6,64]{0,2,1:T(8,128)(2,1)} %bitcast.136), kind=kOutput, calls=%fused_computation.154 | convolution fusion | flops 618332160 | bytes 20865024 | tf_op jit(solution)/shard_map/hqk,khd->qhd/dot_general | solution.py:126
  66.6 8.3 fusion.148
  75.5 9.6 %fusion = f32[6,512]{1,0:T(8,128)} fusion(f32[6,512,1536]{2,1,0:T(8,128)} %get-tuple-element.220, f32[6,512]{1,0:T(8,128)S(1)} %get-tuple-element.219), kind=kLoop, calls=%fused_computation.25 | loop fusion | flops 9434112 | bytes 18898944 | tf_op jit(solution)/shard_map/reduce_sum | solution.py:123
  90.8 8.9 %fusion.92 = bf16[6,64,512]{2,1,0:T(8,128)(2,1)} fusion(f32[6,512,1536]{2,1,0:T(8,128)} %get-tuple-element.220, f32[6,512]{1,0:T(8,128)S(1)} %copy-done.65, f32[6,512]{1,0:T(8,128)S(1)} %copy-done.59, bf16[2048,6,64]{0,2,1:T(8,128)(2,1)S(1)} %bitcast.138), kind=kOutput, calls=%fused_computation.155 | convolution fusion | flops 618332160 | bytes 20865024 | tf_op jit(solution)/shard_map/hqk,khd->qhd/dot_general | solution.py:126
  104.3 9.7 %fusion.55 = f32[1536,6,64]{0,2,1:T(8,128)} fusion(bf16[512,6,64]{0,2,1:T(8,128)(2,1)S(1)} %bitcast.161, f32[6,512,1536]{2,1,0:T(8,128)} %get-tuple-element.220, f32[6,512]{1,0:T(8,128)S(1)} %log_add_fusion.3), kind=kOutput, calls=%fused_computation.114 | convolution fusion | flops 613416960 | bytes 21639168 | tf_op jit(solution)/shard_map/hqk,qhd->khd/dot_general | solution.py:193
  114.0 12.4 %multiply_reduce_fusion.3 = (f32[6,512]{1,0:T(8,128)S(1)}, f32[6,512,1536]{2,1,0:T(8,128)}) fusion(f32[6,512,1536]{2,1,0:T(8,128)} %get-tuple-element.220, f32[6,512]{1,0:T(8,128)S(1)} %log_add_fusion.3, bf16[512,6,64]{0,2,1:T(8,128)(2,1)S(1)} %bitcast.162, bf16[2048,6,64]{0,2,1:T(8,128)(2,1)S(1)} %bitcast.139), kind=kOutput, calls=%fused_computation.11 | convolution fusion | flops 618132480 | bytes 39739392 | tf_op jit(solution)/shard_map/qhd,khd->hqk/dot_general | solution.py:166
  126.5 13.0 %multiply_convert_fusion.3 = bf16[6,512,1536]{2,1,0:T(8,128)(2,1)S(1)} fusion(f32[6,512,1536]{2,1,0:T(8,128)} %get-tuple-element.228, f32[6,512,1536]{2,1,0:T(8,128)} %get-tuple-element.220, f32[6,512]{1,0:T(8,128)S(1)} %get-tuple-element.227, f32[6,512]{1,0:T(8,128)S(1)} %log_add_fusion.3), kind=kLoop, calls=%fused_computation.10 | loop fusion | flops 18874368 | bytes 47210496 | tf_op jit(solution)/shard_map/convert_element_type | solution.py:173
  146.5 8.3 fusion.145
  155.4 9.6 %fusion.3 = f32[6,512]{1,0:T(8,128)} fusion(f32[6,512,1536]{2,1,0:T(8,128)} %get-tuple-element.214, f32[6,512]{1,0:T(8,128)S(1)} %get-tuple-element.213), kind=kLoop, calls=%fused_computation.28 | loop fusion | flops 9434112 | bytes 18898944 | tf_op jit(solution)/shard_map/reduce_sum | solution.py:123
  165.8 13.1 %multiply_reduce_fusion = (f32[6,512]{1,0:T(8,128)S(1)}, f32[6,512,1536]{2,1,0:T(8,128)}) fusion(f32[6,512,1536]{2,1,0:T(8,128)} %get-tuple-element.214, f32[6,512]{1,0:T(8,128)S(1)} %log_add_fusion, bf16[512,6,64]{0,2,1:T(8,128)(2,1)} %bitcast.155, bf16[1536,6,64]{0,2,1:T(8,128)(2,1)} %bitcast.151), kind=kOutput, calls=%fused_computation.2 | convolution fusion | flops 618132480 | bytes 39346176 | tf_op jit(solution)/shard_map/qhd,khd->hqk/dot_general | solution.py:166
  178.9 13.3 %multiply_convert_fusion = bf16[6,512,1536]{2,1,0:T(8,128)(2,1)S(1)} fusion(f32[6,512,1536]{2,1,0:T(8,128)} %get-tuple-element.222, f32[6,512,1536]{2,1,0:T(8,128)} %get-tuple-element.214, f32[6,512]{1,0:T(8,128)S(1)} %get-tuple-element.221, f32[6,512]{1,0:T(8,128)S(1)} %log_add_fusion), kind=kLoop, calls=%fused_computation.1 | loop fusion | flops 18874368 | bytes 47210496 | tf_op jit(solution)/shard_map/convert_element_type | solution.py:173
  196.3 9.0 %fusion.146 = (f32[6,512]{1,0:T(8,128)}, f32[6,512,1536]{2,1,0:T(8,128)}) fusion(bf16[2048,6,48]{0,2,1:T(8,128)(2,1)S(1)} %copy-done.14, bf16[2048,6,16]{0,2,1:T(8,128)(2,1)S(1)} %copy-done.29, bf16[2048,6,48]{0,2,1:T(8,128)(2,1)S(1)} %slice.567, bf16[2048,6,16]{0,2,1:T(8,128)(2,1)S(1)} %copy-done.10, pred[512,1536]{1,0:T(8,128)(4,1)S(1)} %copy-done.55), kind=kOutput, calls=%fused_computation.243 | convolution fusion | flops 621278208 | bytes 22818816 | tf_op jit(solution)/shard_map/qhd,khd->hqk/dot_general | solution.py:107
  205.3 9.6 %fusion.2 = f32[6,512]{1,0:T(8,128)} fusion(f32[6,512,1536]{2,1,0:T(8,128)} %get-tuple-element.216, f32[6,512]{1,0:T(8,128)} %get-tuple-element.215), kind=kLoop, calls=%fused_computation.27 | loop fusion | flops 9434112 | bytes 18898944 | tf_op jit(solution)/shard_map/reduce_sum | solution.py:123
  215.7 12.7 %multiply_reduce_fusion.1 = (f32[6,512]{1,0:T(8,128)S(1)}, f32[6,512,1536]{2,1,0:T(8,128)}) fusion(f32[6,512,1536]{2,1,0:T(8,128)} %get-tuple-element.216, f32[6,512]{1,0:T(8,128)S(1)} %log_add_fusion.1, bf16[512,6,64]{0,2,1:T(8,128)(2,1)} %bitcast.157, bf16[1536,6,64]{0,2,1:T(8,128)(2,1)} %bitcast.149), kind=kOutput, calls=%fused_computation.5 | convolution fusion | flops 618132480 | bytes 39346176 | tf_op jit(solution)/shard_map/qhd,khd->hqk/dot_general | solution.py:166
  228.4 13.5 %multiply_convert_fusion.1 = bf16[6,512,1536]{2,1,0:T(8,128)(2,1)S(1)} fusion(f32[6,512,1536]{2,1,0:T(8,128)} %get-tuple-element.224, f32[6,512,1536]{2,1,0:T(8,128)} %get-tuple-element.216, f32[6,512]{1,0:T(8,128)S(1)} %get-tuple-element.223, f32[6,512]{1,0:T(8,128)S(1)} %log_add_fusion.1), kind=kLoop, calls=%fused_computation.4 | loop fusion | flops 18874368 | bytes 47210496 | tf_op jit(solution)/shard_map/convert_element_type | solution.py:173
  245.8 12.6 %multiply_reduce_fusion.2 = (f32[6,512]{1,0:T(8,128)S(1)}, f32[6,512,1536]{2,1,0:T(8,128)}) fusion(f32[6,512,1536]{2,1,0:T(8,128)} %get-tuple-element.218, f32[6,512]{1,0:T(8,128)S(1)} %copy-done.57, bf16[512,6,64]{0,2,1:T(8,128)(2,1)} %bitcast.159, bf16[2048,6,64]{0,2,1:T(8,128)(2,1)} %bitcast.137), kind=kOutput, calls=%fused_computation.8 | convolution fusion | flops 618132480 | bytes 39739392 | tf_op jit(solution)/shard_map/qhd,khd->hqk/dot_general | solution.py:166
  258.4 13.0 %multiply_convert_fusion.2 = bf16[6,512,1536]{2,1,0:T(8,128)(2,1)S(1)} fusion(f32[6,512,1536]{2,1,0:T(8,128)} %get-tuple-element.226, f32[6,512,1536]{2,1,0:T(8,128)} %get-tuple-element.218, f32[6,512]{1,0:T(8,128)S(1)} %get-tuple-element.225, f32[6,512]{1,0:T(8,128)S(1)} %copy-done.57), kind=kLoop, calls=%fused_computation.7 | loop fusion | flops 18874368 | bytes 47210496 | tf_op jit(solution)/shard_map/convert_element_type | solution.py:173
  289.8 8.1 fusion.82
  298.0 8.3 fusion.76
  306.3 8.1 fusion.70
  331.8 35.3 %multiply_convert_fusion.4 = (bf16[2048,1536]{1,0:T(8,128)(2,1)}, f32[2048,1536]{1,0:T(8,128)}, f32[2048,1536]{1,0:T(8,128)}) fusion(f32[1536]{0:T(1024)S(1)} %copy-done.71, bf16[768,1536]{1,0:T(8,128)(2,1)S(1)} %copy-done, bf16[2048,768]{1,0:T(8,128)(2,1)} %all-gather.3.cloned.1.call-done, f32[768]{0:T(1024)S(1)} %copy-done.73, f32[768]{0:T(1024)S(1)} %copy-done.74, ...), kind=kOutput, calls=%fused_computation.36 | convolution fusion | flops 5048893440 | bytes 36990976 | tf_op jit(solution)/shard_map/dot_general | solution.py:135
  367.1 16.0 %convert_reduce_fusion = (f32[1536]{0:T(1024)S(1)}, bf16[2048,1536]{1,0:T(8,128)(2,1)}) fusion(f32[2048,1536]{1,0:T(8,128)} %get-tuple-element.170, bf16[2048,768]{1,0:T(8,128)(2,1)S(1)} %copy-done.84, bf16[1536,768]{1,0:T(8,128)(2,1)S(1)} %copy-done.86, f32[2048,1536]{1,0:T(8,128)} %get-tuple-element.210, f32[1536]{0:T(1024)S(1)} %copy-done.71), kind=kOutput, calls=%fused_computation.34 | convolution fusion | flops 4885314048 | bytes 36974592 | tf_op jit(solution)/shard_map/sd,fd->sf/dot_general | solution.py:151
  383.1 7.8 fusion.150
  391.0 8.1 bitcast_reduce_fusion
  399.2 9.6 %fusion.149 = f32[2048,768]{1,0:T(8,128)} fusion(bf16[2048,1536]{1,0:T(8,128)(2,1)} %get-tuple-element.169, bf16[1536,768]{1,0:T(8,128)(2,1)} %param.39), kind=kOutput, calls=%fused_computation.246 | convolution fusion | flops 4831838208 | bytes 14942208 | tf_op jit(solution)/shard_map/dot_general | solution.py:140
  408.9 9.8 %fusion.89 = bf16[6,64,512]{2,1,0:T(8,128)(2,1)} fusion(bf16[1536,6,64]{0,2,1:T(8,128)(2,1)} %bitcast.152, f32[6,512,1536]{2,1,0:T(8,128)} %get-tuple-element.214, f32[6,512]{1,0:T(8,128)S(1)} %copy-done.62, f32[6,512]{1,0:T(8,128)S(1)} %copy-done.61), kind=kOutput, calls=%fused_computation.152 | convolution fusion | flops 618332160 | bytes 20471808 | tf_op jit(solution)/shard_map/hqk,khd->qhd/dot_general | solution.py:126
  450.9 7.2 fusion.134
  458.9 44.1 %all-reduce.13 = (f32[2,768]{1,0:T(2,128)}, f32[2,768]{1,0:T(2,128)}, f32[1,768]{1,0:T(1,128)S(1)}) all-reduce(f32[2,768]{1,0:T(2,128)S(1)} %pad_maximum_fusion.9, f32[2,768]{1,0:T(2,128)S(1)} %pad_maximum_fusion.10, f32[1,768]{1,0:T(1,128)S(1)} %stack.47), channel_id=1, replica_groups=mesh['dp'=16,'tensor'=2] {'dp','tensor'}, use_global_device_ids=true, to_apply=%region_24.25 | all-reduce | flops 3840 | bytes 30720 | tf_op jit(solution)/shard_map/psum | solution.py:229
  505.8 80.8 %all-reduce.14 = (f32[3,384]{1,0:T(4,128)}, f32[1536]{0:T(1024)}) all-reduce(f32[3,384]{1,0:T(4,128)S(1)} %convert_reduce_fusion.1, f32[1536]{0:T(1024)S(1)} %get-tuple-element.229), channel_id=1, replica_groups=mesh['dp'=16,'tensor'=2] {'dp'}, use_global_device_ids=true, to_apply=%region_30.31 | all-reduce | flops 2688 | bytes 21504 | tf_op jit(solution)/shard_map/psum | solution.py:226
  597.9 261.0 %all-reduce.18.cloned.1.call-done = (f32[3,768,384]{1,2,0:T(8,128)}, f32[384,768]{1,0:T(8,128)}, f32[768,1536]{1,0:T(8,128)}, f32[1536,768]{1,0:T(8,128)}) async-done(((f32[3,768,384]{1,2,0:T(8,128)}, f32[384,768]{1,0:T(8,128)}, f32[768,1536]{1,0:T(8,128)}, f32[1536,768]{1,0:T(8,128)}), (f32[3,768,384]{1,2,0:T(8,128)}, f32[384,768]{1,0:T(8,128)}, f32[768,1536]{1,0:T(8,128)}, ...) | async-done | bytes 14155792 | tf_op jit(solution)/shard_map/psum | solution.py:226
  (324 shorter events, 155.8 us)
Async XLA Ops:
  7.2 324.6 %copy-start = (bf16[768,1536]{1,0:T(8,128)(2,1)S(1)}, bf16[768,1536]{1,0:T(8,128)(2,1)}, u32[]{:S(2)}) copy-start(bf16[768,1536]{1,0:T(8,128)(2,1)} %param.37) | copy-start | bytes 7077892
  7.2 17.2 %all-gather.3.cloned.1.call-start = ((), (), s32[]{:S(2)}) async-start(), calls=%async_computation.2 | async-start | bytes 4718592 | tf_op jit(solution)/shard_map/all_gather | solution.py:74
  8.0 91.8 %all-gather.5.cloned.1.call-start = ((), (), s32[]{:S(2)}) async-start(), calls=%async_computation.4 | async-start | bytes 4718592 | tf_op jit(solution)/shard_map/all_gather | solution.py:149
  13.7 573.5 %reduce-scatter.5.cloned.1.call-start = ((), (), s32[]{:S(2)}) async-start(), calls=%async_computation.5 | async-start | bytes 4718592 | tf_op jit(solution)/shard_map/reduce_scatter | solution.py:216
  17.4 11.0 %copy-start.75 = (f32[768]{0:T(1024)}, f32[768]{0:T(1024)S(1)}, u32[]{:S(2)}) copy-start(f32[768]{0:T(1024)S(1)} %get-tuple-element.150) | copy-start | bytes 9220
  17.4 11.1 %copy-start.77 = (f32[768]{0:T(1024)}, f32[768]{0:T(1024)S(1)}, u32[]{:S(2)}) copy-start(f32[768]{0:T(1024)S(1)} %get-tuple-element.232) | copy-start | bytes 9220
  57.2 9.4 %copy-start.8 = (bf16[2048,6,16]{0,2,1:T(8,128)(2,1)S(1)}, bf16[2048,6,16]{0,2,1:T(8,128)(2,1)}, u32[]{:S(2)}) copy-start(bf16[2048,6,16]{0,2,1:T(8,128)(2,1)} %copy-done.7) | copy-start | bytes 1179652
  57.2 9.4 %copy-start.43 = (pred[512,1536]{1,0:T(8,128)(4,1)S(1)}, pred[512,1536]{1,0:T(8,128)(4,1)}, u32[]{:S(2)}) copy-start(pred[512,1536]{1,0:T(8,128)(4,1)} %get-tuple-element.198) | copy-start | bytes 2359300
  104.3 9.7 %copy-start.17 = (bf16[1,2048,384]{1,2,0:T(8,128)(2,1)S(1)}, bf16[1,2048,384]{1,2,0:T(8,128)(2,1)}, u32[]{:S(2)}) copy-start(bf16[1,2048,384]{1,2,0:T(8,128)(2,1)} %slice.432) | copy-start | bytes 4718596
  126.4 13.0 %copy-start.5 = (bf16[2048,6,64]{0,2,1:T(8,128)(2,1)S(1)}, bf16[2048,6,64]{0,2,1:T(8,128)(2,1)}, u32[]{:S(2)}) copy-start(bf16[2048,6,64]{0,2,1:T(8,128)(2,1)} %copy-done.3) | copy-start | bytes 4718596
  178.9 13.4 %copy-start.14 = (bf16[2048,6,48]{0,2,1:T(8,128)(2,1)S(1)}, bf16[2048,6,48]{0,2,1:T(8,128)(2,1)}, u32[]{:S(2)}) copy-start(bf16[2048,6,48]{0,2,1:T(8,128)(2,1)} %copy-done.12) | copy-start | bytes 3538948
  178.9 13.4 %copy-start.29 = (bf16[2048,6,16]{0,2,1:T(8,128)(2,1)S(1)}, bf16[2048,6,16]{0,2,1:T(8,128)(2,1)}, u32[]{:S(2)}) copy-start(bf16[2048,6,16]{0,2,1:T(8,128)(2,1)} %copy-done.27) | copy-start | bytes 1179652
  228.4 13.5 %copy-start.15 = (bf16[2048,6,48]{0,2,1:T(8,128)(2,1)S(1)}, bf16[2048,6,48]{0,2,1:T(8,128)(2,1)}, u32[]{:S(2)}) copy-start(bf16[2048,6,48]{0,2,1:T(8,128)(2,1)} %copy-done.12) | copy-start | bytes 3538948
  228.4 13.5 %copy-start.30 = (bf16[2048,6,16]{0,2,1:T(8,128)(2,1)S(1)}, bf16[2048,6,16]{0,2,1:T(8,128)(2,1)}, u32[]{:S(2)}) copy-start(bf16[2048,6,16]{0,2,1:T(8,128)(2,1)} %copy-done.27) | copy-start | bytes 1179652
  258.4 13.0 %copy-start.6 = (bf16[2048,6,64]{0,2,1:T(8,128)(2,1)S(1)}, bf16[2048,6,64]{0,2,1:T(8,128)(2,1)}, u32[]{:S(2)}) copy-start(bf16[2048,6,64]{0,2,1:T(8,128)(2,1)} %copy-done.3) | copy-start | bytes 4718596
  331.8 35.3 %copy-start.84 = (bf16[2048,768]{1,0:T(8,128)(2,1)S(1)}, bf16[2048,768]{1,0:T(8,128)(2,1)}, u32[]{:S(2)}) copy-start(bf16[2048,768]{1,0:T(8,128)(2,1)} %all-gather.5.cloned.1.call-done) | copy-start | bytes 9437188
  331.8 35.3 %copy-start.86 = (bf16[1536,768]{1,0:T(8,128)(2,1)S(1)}, bf16[1536,768]{1,0:T(8,128)(2,1)}, u32[]{:S(2)}) copy-start(bf16[1536,768]{1,0:T(8,128)(2,1)} %param.39) | copy-start | bytes 7077892
  399.1 191.1 %reduce-scatter.3.cloned.1.call-start = ((), (), s32[]{:S(2)}) async-start(), calls=%async_computation.3 | async-start | bytes 4718592 | tf_op jit(solution)/shard_map/reduce_scatter | solution.py:143
  399.2 9.7 %copy-start.61 = (f32[6,512]{1,0:T(8,128)S(1)}, f32[6,512]{1,0:T(8,128)}, u32[]{:S(2)}) copy-start(f32[6,512]{1,0:T(8,128)} %copy-done.60) | copy-start | bytes 36868
  399.2 9.7 %copy-start.62 = (f32[6,512]{1,0:T(8,128)S(1)}, f32[6,512]{1,0:T(8,128)}, u32[]{:S(2)}) copy-start(f32[6,512]{1,0:T(8,128)} %fusion.3) | copy-start | bytes 36868
  399.2 19.5 %slice-start = ((s8[18874368]{0:T(1024)(128)(4,1)}), s8[4194304]{0:T(1024)(128)(4,1)S(1)}, s32[]{:S(2)}) async-start(s8[18874368]{0:T(1024)(128)(4,1)} %bitcast.132), calls=%async_computation.7 | async-start | bytes 8388608
  399.2 19.5 %slice-start.1 = ((s8[18874368]{0:T(1024)(128)(4,1)}), s8[4194304]{0:T(1024)(128)(4,1)S(1)}, s32[]{:S(2)}) async-start(s8[18874368]{0:T(1024)(128)(4,1)} %bitcast.132), calls=%async_computation.8 | async-start | bytes 8388608
  408.8 9.9 %slice-start.2 = ((s8[18874368]{0:T(1024)(128)(4,1)}), s8[4194304]{0:T(1024)(128)(4,1)S(1)}, s32[]{:S(2)}) async-start(s8[18874368]{0:T(1024)(128)(4,1)} %bitcast.132), calls=%async_computation.9 | async-start | bytes 8388608
  408.8 9.9 %slice-start.3 = ((s8[18874368]{0:T(1024)(128)(4,1)}), s8[4194304]{0:T(1024)(128)(4,1)S(1)}, s32[]{:S(2)}) async-start(s8[18874368]{0:T(1024)(128)(4,1)} %bitcast.132), calls=%async_computation.10 | async-start | bytes 8388608
  408.9 10.3 %slice-start.4 = ((s8[18874368]{0:T(1024)(128)(4,1)}), s8[2097152]{0:T(1024)(128)(4,1)S(1)}, s32[]{:S(2)}) async-start(s8[18874368]{0:T(1024)(128)(4,1)} %bitcast.132), calls=%async_computation.11 | async-start | bytes 4194304
  408.9 10.6 %copy-start.38 = (bf16[1,1536,384]{1,2,0:T(8,128)(2,1)S(1)}, bf16[1,1536,384]{1,2,0:T(8,128)(2,1)}, u32[]{:S(2)}) copy-start(bf16[1,1536,384]{1,2,0:T(8,128)(2,1)} %get-tuple-element.176) | copy-start | bytes 3538948
  408.9 10.6 %copy-start.63 = (f32[6,512]{1,0:T(8,128)S(1)}, f32[6,512]{1,0:T(8,128)}, u32[]{:S(2)}) copy-start(f32[6,512]{1,0:T(8,128)} %get-tuple-element.215) | copy-start | bytes 36868
  408.9 10.6 %copy-start.64 = (f32[6,512]{1,0:T(8,128)S(1)}, f32[6,512]{1,0:T(8,128)}, u32[]{:S(2)}) copy-start(f32[6,512]{1,0:T(8,128)} %fusion.2) | copy-start | bytes 36868
  432.4 426.5 %all-reduce.18.cloned.1.call-start = ((), (), s32[]{:S(2)}) async-start(), calls=%async_computation.6 | async-start | bytes 28311552 | tf_op jit(solution)/shard_map/psum | solution.py:226
  432.7 11.3 %slice-start.11 = ((s8[6291456]{0:T(1024)(128)(4,1)}), s8[4194304]{0:T(1024)(128)(4,1)S(1)}, s32[]{:S(2)}) async-start(s8[6291456]{0:T(1024)(128)(4,1)} %bitcast.171), calls=%async_computation.19 | async-start | bytes 8388608
  432.7 18.2 %slice-start.13 = ((s8[6291456]{0:T(1024)(128)(4,1)}), s8[4194304]{0:T(1024)(128)(4,1)S(1)}, s32[]{:S(2)}) async-start(s8[6291456]{0:T(1024)(128)(4,1)} %bitcast.173), calls=%async_computation.21 | async-start | bytes 8388608
  437.4 13.4 %slice-start.14 = ((s8[6291456]{0:T(1024)(128)(4,1)}), s8[2097152]{0:T(1024)(128)(4,1)S(1)}, s32[]{:S(2)}) async-start(s8[6291456]{0:T(1024)(128)(4,1)} %bitcast.173), calls=%async_computation.22 | async-start | bytes 4194304
  (80 other events, 368.9 us)
Sparse Core Ops, SparseCore 0:
  9.6 14.8 all-gather.2
  26.0 13.2 all-gather.4
  399.2 12.0 reduce-scatter.4
  432.5 12.0 reduce-scatter.2
  458.2 400.6 all-reduce.17
where the time goes:
time: 889 us; the launch traced here: 880 us
  matrix products  295 us (33%)
  waiting for transfers between devices  265 us (30%)
  other arithmetic  137 us (15%)
  blocking collectives  125 us (14%)
  local copies, waits for them, and re-layouts  42 us (5%)
  between operations  15.3 us (2%)
    psum x1, waiting for transfers between devices, shards(): lax.psum((qkv_grad, qkv_bias_grad, out_w_grad, up_grad, up_bias_grad, dow...  261 us
    psum x1, blocking collectives, shards(): lax.psum((qkv_grad, qkv_bias_grad, out_w_grad, up_grad, up_bias_grad, dow...  80.8 us
    convert_element_type x4, other arithmetic, shards(): score_back = (probs * (prob_back - inner)).astype(jnp.bfloat16)  52.8 us
    dot_general x4, matrix products, shards(): jnp.einsum('qhd,khd->hqk', rows_back, value_pad[offset:offset + window],...  51 us
    psum x1, blocking collectives, shards(): lax.psum((gain_grad, shift_grad, bias_grad), ('dp', 'tensor'))  44.1 us
    reduce_sum x4, other arithmetic, shards(): totals = jnp.sum(expanded, -1, keepdims=True)  38.4 us
    dot_general x1, matrix products, shards(): jnp.dot(second, up_weight, preferred_element_type=jnp.float32)  35.3 us
    dot_general x4, matrix products, shards(): jnp.einsum('hqk,qhd->khd', probs.astype(jnp.bfloat16), rows_back, preferr...  34.3 us
  transfers between devices with their start and end apart: 5, of which 2 were waited for; matrix products, arithmetic and copies ran while one was open for 18% of the time, Pallas kernels for 0%

commit v1 on v0

v1 whole, which is shorter than its diff:
```python
import functools
import math

import jax
import jax.numpy as jnp
from jax import lax
from jax.experimental import pallas as pl
from jax.experimental.pallas import tpu as pltpu
from jax.sharding import PartitionSpec as P

HD = 64
ROT = 16
MAXLEN = 1024
BLOCK = 256
PAIR = 2 * HD
ROWS = 512
F32 = jnp.float32
BF16 = jnp.bfloat16


def standard(values):
    center = values - jnp.mean(values, -1, keepdims=True)
    spread = jnp.mean(center * center, -1, keepdims=True)
    inverse = lax.rsqrt(spread + 1e-05)
    return (center * inverse, inverse)


def layout(lengths, owners, index, slot_count):
    mine = owners == index
    sizes = jnp.where(mine, lengths, 0)
    starts = jnp.cumsum(sizes) - sizes
    rows = jnp.arange(slot_count, dtype=jnp.int32)
    covers = mine[None, :] & (starts[None, :] <= rows[:, None])
    begins = jnp.max(jnp.where(covers, starts[None, :], 0), 1)
    filled = rows < jnp.sum(sizes)
    return (jnp.where(filled, begins, rows), filled)


def rotary_tables(places):
    half = ROT // 2
    freq = 10000.0 ** (-jnp.arange(half, dtype=F32) * 2.0 / ROT)
    angles = places.astype(F32)[:, None] * freq[None, :]
    angles = jnp.concatenate([angles, angles], 1)
    rest = jnp.zeros((places.shape[0], HD - ROT), F32)
    cosine = jnp.concatenate([jnp.cos(angles), rest + 1.0], 1)
    sine = jnp.concatenate([jnp.sin(angles), rest], 1)
    return jnp.concatenate([cosine] * 2, 1), jnp.concatenate([sine] * 2, 1)


def dot(a, b, dims):
    return lax.dot_general(a, b, (dims, ((), ())), preferred_element_type=F32)


NN = ((1,), (0,))
NT = ((1,), (1,))
TN = ((0,), (0,))


def attention_kernel(
    low_ref, a_ref, back_ref, start_ref, cos_ref, sin_ref,
    o_ref, da_ref,
    q_s, k_s, v_s, dk_s, dv_s, s_s, dp_s, q2_s, do2_s, top_s, sum_s, mix_s, o2_s, dq2_s,
):
    slots = q_s.shape[0]
    blocks = slots // BLOCK
    lane = lax.broadcasted_iota(jnp.int32, (BLOCK, PAIR), 1)
    within = lane % HD

    def turn(w):
        up = pltpu.roll(w, PAIR - ROT // 2, 1)
        down = pltpu.roll(w, ROT // 2, 1)
        return jnp.where(within < ROT // 2, -up, down)

    def prepare(b, carry):
        rows = pl.ds(pl.multiple_of(b * BLOCK, BLOCK), BLOCK)
        cosine = cos_ref[rows, :]
        sine = sin_ref[rows, :]
        q = a_ref[0, rows, :]
        k = a_ref[1, rows, :]
        q = (q * cosine + turn(q) * sine).astype(BF16)
        q_s[rows, :] = (q.astype(F32) * (1.0 / math.sqrt(HD))).astype(BF16)
        k_s[rows, :] = (k * cosine + turn(k) * sine).astype(BF16)
        v_s[rows, :] = a_ref[2, rows, :].astype(BF16)
        dk_s[rows, :] = jnp.zeros((BLOCK, PAIR), F32)
        dv_s[rows, :] = jnp.zeros((BLOCK, PAIR), F32)
        return carry

    lax.fori_loop(0, blocks, prepare, 0)

    def query_block(i, carry):
        rows = pl.ds(pl.multiple_of(i * BLOCK, BLOCK), BLOCK)
        low = low_ref[i]
        none = jnp.zeros((BLOCK, PAIR), BF16)
        q = q_s[rows, :]
        back = back_ref[rows, :]
        q2_s[:BLOCK, :] = jnp.where(lane < HD, q, none)
        q2_s[BLOCK:, :] = jnp.where(lane < HD, none, q)
        do2_s[:BLOCK, :] = jnp.where(lane < HD, back, none)
        do2_s[BLOCK:, :] = jnp.where(lane < HD, none, back)
        start = start_ref[rows, :]
        start2 = jnp.concatenate([start, start], 0)
        row = lax.broadcasted_iota(jnp.int32, (BLOCK, 1), 0) + i * BLOCK
        row2 = jnp.concatenate([row, row], 0)
        top_s[...] = jnp.full(top_s.shape, -1e30, F32)
        sum_s[...] = jnp.zeros(sum_s.shape, F32)
        mix_s[...] = jnp.zeros(mix_s.shape, F32)
        o2_s[...] = jnp.zeros(o2_s.shape, F32)
        dq2_s[...] = jnp.zeros(dq2_s.shape, F32)
        column = lax.broadcasted_iota(jnp.int32, (2 * BLOCK, BLOCK), 1)

        def score(j, c):
            keys = pl.ds(pl.multiple_of(j * BLOCK, BLOCK), BLOCK)
            s = dot(q2_s[...], k_s[keys, :], NT)
            place = column + j * BLOCK
            s = jnp.where((place >= start2) & (place <= row2), s, -1e30)
            s_s[j - low] = s
            dp_s[j - low] = dot(do2_s[...], v_s[keys, :], NT)
            top_s[...] = jnp.maximum(top_s[...], jnp.maximum(s[:, :128], s[:, 128:]))
            return c

        lax.fori_loop(low, i + 1, score, 0)
        top = jnp.max(top_s[...], -1, keepdims=True)

        def expand(j, c):
            p = jnp.exp(s_s[j - low] - top)
            s_s[j - low] = p
            m = p * dp_s[j - low]
            sum_s[...] += p[:, :128] + p[:, 128:]
            mix_s[...] += m[:, :128] + m[:, 128:]
            return c

        lax.fori_loop(low, i + 1, expand, 0)
        total = jnp.sum(sum_s[...], -1, keepdims=True)
        inverse = 1.0 / total
        inner = jnp.sum(mix_s[...], -1, keepdims=True) * inverse

        def apply(j, c):
            keys = pl.ds(pl.multiple_of(j * BLOCK, BLOCK), BLOCK)
            p = s_s[j - low] * inverse
            ds = (p * (dp_s[j - low] - inner)).astype(BF16)
            p = p.astype(BF16)
            o2_s[...] += dot(p, v_s[keys, :], NN)
            dq2_s[...] += dot(ds, k_s[keys, :], NN)
            dk_s[keys, :] += dot(ds, q2_s[...], TN)
            dv_s[keys, :] += dot(p, do2_s[...], TN)
            return c

        lax.fori_loop(low, i + 1, apply, 0)
        o_ref[rows, :] = jnp.where(lane < HD, o2_s[:BLOCK, :], o2_s[BLOCK:, :]).astype(BF16)
        dq = jnp.where(lane < HD, dq2_s[:BLOCK, :], dq2_s[BLOCK:, :]) * (1.0 / math.sqrt(HD))
        da_ref[0, rows, :] = (dq * cos_ref[rows, :] - turn(dq) * sin_ref[rows, :]).astype(BF16)
        return carry

    lax.fori_loop(0, blocks, query_block, 0)

    def finish(b, carry):
        rows = pl.ds(pl.multiple_of(b * BLOCK, BLOCK), BLOCK)
        dk = dk_s[rows, :]
        da_ref[1, rows, :] = (dk * cos_ref[rows, :] - turn(dk) * sin_ref[rows, :]).astype(BF16)
        da_ref[2, rows, :] = dv_s[rows, :].astype(BF16)
        return carry

    lax.fori_loop(0, blocks, finish, 0)


def attention(low, projected, back, start, cosine, sine):
    _, slots, width = projected.shape
    pairs = width // PAIR
    span = MAXLEN // BLOCK + 1
    return pl.pallas_call(
        attention_kernel,
        grid_spec=pltpu.PrefetchScalarGridSpec(
            num_scalar_prefetch=1,
            grid=(pairs,),
            in_specs=[
                pl.BlockSpec((3, slots, PAIR), lambda g, low: (0, 0, g)),
                pl.BlockSpec((slots, PAIR), lambda g, low: (0, g)),
                pl.BlockSpec((slots, 1), lambda g, low: (0, 0)),
                pl.BlockSpec((slots, PAIR), lambda g, low: (0, 0)),
                pl.BlockSpec((slots, PAIR), lambda g, low: (0, 0)),
            ],
            out_specs=[
                pl.BlockSpec((slots, PAIR), lambda g, low: (0, g)),
                pl.BlockSpec((3, slots, PAIR), lambda g, low: (0, 0, g)),
            ],
            scratch_shapes=[
                pltpu.VMEM((slots, PAIR), BF16),
                pltpu.VMEM((slots, PAIR), BF16),
                pltpu.VMEM((slots, PAIR), BF16),
                pltpu.VMEM((slots, PAIR), F32),
                pltpu.VMEM((slots, PAIR), F32),
                pltpu.VMEM((span, 2 * BLOCK, BLOCK), F32),
                pltpu.VMEM((span, 2 * BLOCK, BLOCK), F32),
                pltpu.VMEM((2 * BLOCK, PAIR), BF16),
                pltpu.VMEM((2 * BLOCK, PAIR), BF16),
                pltpu.VMEM((2 * BLOCK, PAIR), F32),
                pltpu.VMEM((2 * BLOCK, PAIR), F32),
                pltpu.VMEM((2 * BLOCK, PAIR), F32),
                pltpu.VMEM((2 * BLOCK, PAIR), F32),
                pltpu.VMEM((2 * BLOCK, PAIR), F32),
            ],
        ),
        out_shape=[
            jax.ShapeDtypeStruct((slots, width), BF16),
            jax.ShapeDtypeStruct((3, slots, width), BF16),
        ],
        compiler_params=pltpu.CompilerParams(vmem_limit_bytes=52 * 2**20),
        cost_estimate=pl.CostEstimate(
            flops=24 * slots * MAXLEN * width, bytes_accessed=24 * slots * width,
            transcendentals=slots * MAXLEN * width // HD,
        ),
        name="attention",
    )(low, projected, back, start, cosine, sine)


def feed_kernel(h_ref, dy_ref, up_ref, bias_ref, down_ref,
                part_ref, dh_ref, dup_ref, dbias_ref, ddown_ref, up_s, down_s, part_s, dh_s):
    slots = h_ref.shape[0]
    step = pl.program_id(0)
    last = pl.num_programs(0) - 1
    up_s[...] = jnp.zeros(up_s.shape, F32)
    down_s[...] = jnp.zeros(down_s.shape, F32)
    dbias_ref[...] = jnp.zeros(dbias_ref.shape, F32)

    @pl.when(step == 0)
    def _():
        part_s[...] = jnp.zeros(part_s.shape, F32)
        dh_s[...] = jnp.zeros(dh_s.shape, F32)

    def body(b, carry):
        rows = pl.ds(pl.multiple_of(b * ROWS, ROWS), ROWS)
        h = h_ref[rows, :]
        dy = dy_ref[rows, :]
        u = dot(h, up_ref[...], NN) + bias_ref[...].astype(F32)
        dg = dot(dy, down_ref[...], NT)
        phi = 0.5 * (1.0 + lax.erf(u * math.sqrt(0.5)))
        g = (u * phi).astype(BF16)
        slope = phi + u * (jnp.exp(-0.5 * (u * u)) * (1.0 / math.sqrt(2.0 * math.pi)))
        du = (slope * dg).astype(BF16)
        part_s[rows, :] += dot(g, down_ref[...], NN)
        down_s[...] += dot(g, dy, TN)
        dh_s[rows, :] += dot(du, up_ref[...], NT)
        up_s[...] += dot(h, du, TN)
        dbias_ref[...] += jnp.sum(du.astype(F32), 0, keepdims=True)
        return carry

    lax.fori_loop(0, slots // ROWS, body, 0)
    dup_ref[...] = up_s[...].astype(dup_ref.dtype)
    ddown_ref[...] = down_s[...].astype(ddown_ref.dtype)

    @pl.when(step == last)
    def _():
        part_ref[...] = part_s[...].astype(part_ref.dtype)
        dh_ref[...] = dh_s[...].astype(dh_ref.dtype)


def feed(h, dy, up, bias, down):
    slots, width = h.shape
    hidden = up.shape[1]
    tile = 256
    whole = lambda t: (0, 0)
    return pl.pallas_call(
        feed_kernel,
        grid=(hidden // tile,),
        in_specs=[
            pl.BlockSpec((slots, width), whole, pipeline_mode=pl.Buffered(1)),
            pl.BlockSpec((slots, width), whole, pipeline_mode=pl.Buffered(1)),
            pl.BlockSpec((width, tile), lambda t: (0, t)),
            pl.BlockSpec((1, tile), lambda t: (0, t)),
            pl.BlockSpec((tile, width), lambda t: (t, 0)),
        ],
        out_specs=[
            pl.BlockSpec((slots, width), whole, pipeline_mode=pl.Buffered(1)),
            pl.BlockSpec((slots, width), whole, pipeline_mode=pl.Buffered(1)),
            pl.BlockSpec((width, tile), lambda t: (0, t)),
            pl.BlockSpec((1, tile), lambda t: (0, t)),
            pl.BlockSpec((tile, width), lambda t: (t, 0)),
        ],
        scratch_shapes=[
            pltpu.VMEM((width, tile), F32),
            pltpu.VMEM((tile, width), F32),
            pltpu.VMEM((slots, width), F32),
            pltpu.VMEM((slots, width), F32),
        ],
        out_shape=[
            jax.ShapeDtypeStruct((slots, width), F32),
            jax.ShapeDtypeStruct((slots, width), F32),
            jax.ShapeDtypeStruct((width, hidden), BF16),
            jax.ShapeDtypeStruct((1, hidden), F32),
            jax.ShapeDtypeStruct((hidden, width), BF16),
        ],
        compiler_params=pltpu.CompilerParams(vmem_limit_bytes=56 * 2**20),
        cost_estimate=pl.CostEstimate(
            flops=12 * slots * width * hidden, bytes_accessed=22 * 2**20,
            transcendentals=2 * slots * hidden,
        ),
        name="feed",
    )(h, dy, up, bias, down)


def shards(
    tokens,
    out_cot,
    norm_gain,
    norm_bias,
    qkv_weight,
    qkv_bias,
    out_weight,
    out_bias,
    up_weight,
    up_bias,
    down_weight,
    seq_lengths,
    seq_owner,
):
    rows_local = tokens.shape[0]
    slots = rows_local * lax.axis_size("tensor")
    half_index = lax.axis_index("tensor")
    start, filled = layout(seq_lengths, seq_owner, lax.axis_index("dp"), slots)
    places = jnp.arange(slots, dtype=jnp.int32) - start
    valid_local = lax.dynamic_slice_in_dim(filled, half_index * rows_local, rows_local, 0)
    gains = norm_gain.astype(F32)
    shifts = norm_bias.astype(F32)
    x = tokens.astype(F32)
    whole_rows = lax.all_gather(tokens, "tensor", axis=0, tiled=True)
    cot_local = out_cot * valid_local[:, None].astype(BF16)
    cot = lax.all_gather(cot_local, "tensor", axis=0, tiled=True)
    unit_rows, inverse_rows = standard(whole_rows.astype(F32))
    first = (unit_rows * gains[0] + shifts[0]).astype(BF16)
    second = (unit_rows * gains[1] + shifts[1]).astype(BF16)

    feed_part, second_back, up_grad, up_bias_grad, down_grad = feed(
        second, cot, up_weight, up_bias[None, :], down_weight
    )
    up_sum, down_sum = lax.psum((up_grad, down_grad), "dp")

    projected = (
        jnp.einsum("sd,cde->cse", first, qkv_weight, preferred_element_type=F32)
        + qkv_bias.astype(F32)[:, None, :]
    )
    attended_back = dot(cot, out_weight, NT).astype(BF16)
    cosine, sine = rotary_tables(places)
    attended, qkv_delta = attention(
        start[::BLOCK] // BLOCK, projected, attended_back, start[:, None], cosine, sine
    )

    partial_value = feed_part + dot(attended, out_weight, NN)
    summed = lax.psum_scatter(
        partial_value.astype(BF16), "tensor", scatter_dimension=0, tiled=True
    ).astype(F32)
    biases = out_bias.astype(F32)
    mixed = (x + summed + biases[0] + biases[1]).astype(BF16)
    out_w_grad = dot(attended, cot, TN)
    qkv_grad = jnp.einsum("sd,cse->cde", first, qkv_delta, preferred_element_type=F32)
    qkv_bias_grad = jnp.sum(qkv_delta.astype(F32), 1)
    first_back = jnp.einsum("cse,cde->sd", qkv_delta, qkv_weight, preferred_element_type=F32)
    combined = gains[0] * first_back + gains[1] * second_back
    combined_sum = lax.psum_scatter(
        combined.astype(BF16), "tensor", scatter_dimension=0, tiled=True
    ).astype(F32)

    gain_grad = jnp.stack(
        [jnp.sum(first_back * unit_rows, 0), jnp.sum(second_back * unit_rows, 0)], 0
    )
    shift_grad = jnp.stack([jnp.sum(first_back, 0), jnp.sum(second_back, 0)], 0)
    bias_grad = jnp.sum(cot_local.astype(F32), 0)

    qkv_grad16, out_grad16, up_sum, down_sum = lax.optimization_barrier(
        (qkv_grad.astype(BF16), out_w_grad.astype(BF16), up_sum, down_sum)
    )
    width = tokens.shape[1]
    shared = jnp.concatenate([gain_grad, shift_grad, bias_grad[None]], 0).reshape(-1)
    shared = lax.psum(shared, "tensor")
    vectors = jnp.concatenate([shared, qkv_bias_grad.reshape(-1), up_bias_grad.reshape(-1)])
    qkv_sum, out_sum, vector_sum = lax.psum((qkv_grad16, out_grad16, vectors), "dp")
    shared_sum = vector_sum[: 5 * width].reshape(5, width)
    qkv_bias_sum = vector_sum[5 * width : 5 * width + qkv_bias.size].reshape(qkv_bias.shape)
    up_bias_sum = vector_sum[5 * width + qkv_bias.size :]

    unit_local = lax.dynamic_slice_in_dim(unit_rows, half_index * rows_local, rows_local, 0)
    inverse_local = lax.dynamic_slice_in_dim(inverse_rows, half_index * rows_local, rows_local, 0)
    average = jnp.mean(combined_sum, -1, keepdims=True)
    along = jnp.mean(combined_sum * unit_local, -1, keepdims=True)
    x_back = inverse_local * (combined_sum - average - unit_local * along)
    tokens_grad = (cot_local.astype(F32) + x_back).astype(BF16)
    return (
        mixed,
        tokens_grad,
        shared_sum[:2],
        shared_sum[2:4],
        qkv_sum.astype(F32),
        qkv_bias_sum,
        out_sum.astype(F32),
        jnp.stack([shared_sum[4], shared_sum[4]], 0),
        up_sum.astype(F32),
        up_bias_sum,
        down_sum.astype(F32),
    )

def solution(mesh):
    return jax.shard_map(
        shards,
        mesh=mesh,
        in_specs=(
            P(("dp", "tensor"), None),
            P(("dp", "tensor"), None),
            P(),
            P(),
            P(None, None, "tensor"),
            P(None, "tensor"),
            P("tensor", None),
            P(),
            P(None, "tensor"),
            P("tensor"),
            P("tensor", None),
            P(),
            P(),
        ),
        out_specs=(
            P(("dp", "tensor"), None),
            P(("dp", "tensor"), None),
            P(),
            P(),
            P(None, None, "tensor"),
            P(None, "tensor"),
            P("tensor", None),
            P(),
            P(None, "tensor"),
            P("tensor"),
            P("tensor", None),
        ),
        check_vma=False,
    )
```

time: 889 us -> 451 us (0.51)
  matrix products: 295 us -> 42 us
  waiting for transfers between devices: 265 us -> 132 us
  Pallas kernels: 0 us -> 127 us
  other arithmetic: 137 us -> 42.1 us
  blocking collectives: 125 us -> 79.4 us
  local copies, waits for them, and re-layouts: 42 us -> 13 us
    dot_general x36 -> x6, matrix products: 295 us -> 42 us  [the longest x3 15.7 us: dot(): return lax.dot_general(a, b, (dims, ((), ())), preferred_element_type=F32)]
    psum x1 -> x2, waiting for transfers between devices: 261 us -> 122 us  [the longest x1 63.6 us: shards(): lax.psum((qkv_grad16, out_grad16, vectors), 'dp')]
    pallas_call x0 -> x2, Pallas kernels: none -> 127 us  [the longest x1 77.9 us: attention(): pl.pallas_call(attention_kernel, grid_spec=pltpu.PrefetchScalarGridSpec(n...]
    psum x2, blocking collectives: 125 us -> 79.4 us  [the longest x1 76 us: shards(): lax.psum((qkv_grad16, out_grad16, vectors), 'dp')]
    convert_element_type x13 -> x12, other arithmetic: 61.8 us -> 19.7 us  [the longest x1 4.71 us: shards(): up_sum.astype(F32)]
    reduce_sum x7 -> x2, other arithmetic: 46.2 us -> 6 us  [the longest x1 3.03 us: shards(): qkv_bias_grad = jnp.sum(qkv_delta.astype(F32), 1)]
    unnamed x214 -> x35, local copies, waits for them, and re-layouts: 20.9 us -> 6.51 us
  transfers between devices with their start and end apart: 5 -> 6, of which waited for: 2 -> 3; matrix products, arithmetic and copies ran while one was open for 18% -> 20% of each run, Pallas kernels for 0% -> 17%
where the time goes in v1:
time: 451 us; the launch traced here: 450 us
  waiting for transfers between devices  132 us (29%)
  Pallas kernels  127 us (28%)
  blocking collectives  79.4 us (18%)
  other arithmetic  42.1 us (9%)
  matrix products  42 us (9%)
  between operations  14.5 us (3%)
  local copies, waits for them, and re-layouts  13 us (3%)
    pallas_call x1, Pallas kernels, attention(): pl.pallas_call(attention_kernel, grid_spec=pltpu.PrefetchScalarGridSpec(n...  77.9 us
    psum x1, blocking collectives, shards(): lax.psum((qkv_grad16, out_grad16, vectors), 'dp')  76 us
    psum x1, waiting for transfers between devices, shards(): lax.psum((qkv_grad16, out_grad16, vectors), 'dp')  63.6 us
    psum x1, waiting for transfers between devices, shards(): up_sum, down_sum = lax.psum((up_grad, down_grad), 'dp')  58.6 us
    pallas_call x1, Pallas kernels, feed(): pl.pallas_call(feed_kernel, grid=(hidden // tile,), in_specs=[pl.BlockSpe...  49.1 us
    dot_general x3, matrix products, dot(): return lax.dot_general(a, b, (dims, ((), ())), preferred_element_type=F32)  15.7 us
    dot_general x1, matrix products, shards(): jnp.einsum('cse,cde->sd', qkv_delta, qkv_weight, preferred_element_type=F32)  10.5 us
  transfers between devices with their start and end apart: 6, of which 3 were waited for; matrix products, arithmetic and copies ran while one was open for 20% of the time, Pallas kernels for 17%

profile of v1, /device:TPU:0, one launch (start us, length us, event | category | flops | bytes accessed | tf_op | source)
XLA Modules:
  0.0 450.3 jit_solution(7602302385879542454)
XLA Ops:
  7.3 0.7 all-gather.3.cloned.1.call-update
  9.0 1.3 fusion.16
  11.0 3.0 convert_reduce_fusion.3
  16.3 1.3 copy.45
  17.6 1.3 copy.44
  19.2 5.0 %pad_maximum_fusion = (f32[2048,128]{1,0:T(8,128)}, f32[2048,128]{1,0:T(8,128)}) fusion(f32[2048,48]{1,0:T(8,128)S(1)} %add.115, f32[2048,16]{1,0:T(8,128)} %copy.45, f32[2048,48]{1,0:T(8,128)S(1)} %broadcast_in_dim.23, f32[2048,16]{1,0:T(8,128)S(1)} %copy.47), kind=kLoop, calls=%fused_computation.31 | loop fusion | flops 1572864 | bytes 3145728 | tf_op jit(solution)/shard_map/concatenate | solution.py:47
  24.2 0.7 iota_select_fusion.start_ref
  25.0 2.5 convert_reduce_fusion.1
  27.8 1.1 fusion.2
  28.9 2.4 add_convert_fusion.2.h_ref
  31.3 8.6 %all-gather.5.cloned.1.call-done.dy_ref = bf16[2048,768]{1,0:T(8,128)(2,1)} async-done(((bf16[1024,768]{1,0:T(8,128)(2,1)}), bf16[2048,768]{1,0:T(8,128)(2,1)}) %all-gather.5.cloned.1.call-update) | async-done | bytes 3145744 | tf_op jit(solution)/shard_map/all_gather | solution.py:327
  39.9 49.1 %feed.1 = (f32[2048,768]{1,0:T(8,128)}, f32[2048,768]{1,0:T(8,128)}, bf16[768,1536]{1,0:T(8,128)(2,1)}, f32[1,1536]{1,0:T(1,128)}, bf16[1536,768]{1,0:T(8,128)(2,1)}) custom-call(bf16[2048,768]{1,0:T(8,128)(2,1)} %add_convert_fusion.2.h_ref, bf16[2048,768]{1,0:T(8,128)(2,1)} %all-gather.5.cloned.1.call-done.dy_ref, bf16[768,1536]{1,0:T(8,128)(2,1)} %up_ref.1, ...), custom_call_target="tpu_custom_call" | custom-call | flops 28991029248 | bytes 23068672 | tf_op jit(solution)/shard_map/feed/pallas_call | solution.py:262
  90.1 5.0 %convolution_convert_fusion.back_ref = bf16[2048,384]{1,0:T(8,128)(2,1)} fusion(bf16[2048,768]{1,0:T(8,128)(2,1)} %all-gather.5.cloned.1.call-done.dy_ref, bf16[384,768]{1,0:T(8,128)(2,1)S(1)} %copy-done.9), kind=kOutput, calls=%fused_computation.28 | convolution fusion | flops 1208745984 | bytes 5308416 | tf_op jit(solution)/shard_map/dot_general | solution.py:51
  95.1 7.3 %add_bitcast_fusion.a_ref = f32[3,2048,384]{2,1,0:T(8,128)} fusion(f32[3,384]{1,0:T(4,128)S(1)} %convert_element_type.91, bf16[3,768,384]{2,1,0:T(8,128)(2,1)S(1)} %copy-done, bf16[2048,768]{1,0:T(8,128)(2,1)S(1)} %copy-done.2, f32[768]{0:T(1024)S(1)} %get-tuple-element.98, f32[768]{0:T(1024)S(1)} %get-tuple-element.122, f32[2048]{0:T(1024)S(1)} %add_rsqrt_fusion, ...), kind=kOutput, calls=%fused_computation.1 | convolution fusion | flops 3635675136 | bytes 14379520 | tf_op jit(solution)/shard_map/sd,cde->cse/dot_general | solution.py:338
  102.4 77.9 %attention.1 = (bf16[2048,384]{1,0:T(8,128)(2,1)}, bf16[3,2048,384]{2,1,0:T(8,128)(2,1)}) custom-call(s32[8]{0:T(128)S(1)} %and_select_fusion.low_ref, f32[3,2048,384]{2,1,0:T(8,128)} %add_bitcast_fusion.a_ref, bf16[2048,384]{1,0:T(8,128)(2,1)} %convolution_convert_fusion.back_ref, s32[2048,1]{1,0:T(8,128)S(1)} %iota_select_fusion.start_ref, ...), custom_call_target="tpu_custom_call" | custom-call | flops 19327352832 | bytes 18874368 | tf_op jit(solution)/shard_map/attention/pallas_call | solution.py:170
  180.3 10.5 %fusion.19 = (f32[768]{0:T(1024)S(1)}, f32[768]{0:T(1024)S(1)}, bf16[2048,768]{1,0:T(8,128)(2,1)}, f32[768]{0:T(1024)S(1)}, f32[768]{0:T(1024)S(1)}, /*index=5*/f32[2048,768]{1,0:T(8,128)}) fusion(f32[2048,768]{1,0:T(8,128)} %get-tuple-element.25, f32[2048]{0:T(1024)S(1)} %add_rsqrt_fusion, f32[2048]{0:T(1024)S(1)} %broadcast_multiply_fusion.2, ...), kind=kOutput, calls=%fused_computation.69 | convolution fusion | flops 3644322816 | bytes 25397248 | tf_op jit(solution)/shard_map/cse,cde->sd/dot_general | solution.py:356
  190.9 1.3 copy-done.8
  192.3 6.5 %add_convert_fusion = bf16[2048,768]{1,0:T(8,128)(2,1)} fusion(f32[2048,768]{1,0:T(8,128)} %get-tuple-element.22, bf16[2048,384]{1,0:T(8,128)(2,1)S(1)} %copy-done.8, bf16[384,768]{1,0:T(8,128)(2,1)} %param.19), kind=kOutput, calls=%fused_computation.14 | convolution fusion | flops 1211105280 | bytes 11599872 | tf_op jit(solution)/shard_map/dot_general | solution.py:51
  199.0 4.3 convolution_convert_fusion.1
  203.3 8.5 %convert_bitcast_fusion = bf16[3,768,384]{1,2,0:T(8,128)(2,1)} fusion(bf16[3,2048,384]{2,1,0:T(8,128)(2,1)} %get-tuple-element.24, bf16[2048,768]{1,0:T(8,128)(2,1)S(1)} %copy-done.3, f32[768]{0:T(1024)S(1)} %get-tuple-element.98, f32[768]{0:T(1024)S(1)} %get-tuple-element.122, f32[2048]{0:T(1024)S(1)} %add_rsqrt_fusion, f32[2048]{0:T(1024)S(1)} %broadcast_multiply_fusion.2), kind=kOutput, calls=%fused_computation.29 | convolution fusion | flops 3634200576 | bytes 9656320 | tf_op jit(solution)/shard_map/sd,cse->cde/dot_general | solution.py:354
  211.8 58.6 %all-reduce.7.cloned.1.call-done = (bf16[768,1536]{1,0:T(8,128)(2,1)}, bf16[1536,768]{1,0:T(8,128)(2,1)}) async-done(((bf16[768,1536]{1,0:T(8,128)(2,1)}, bf16[1536,768]{1,0:T(8,128)(2,1)}), (bf16[768,1536]{1,0:T(8,128)(2,1)}, bf16[1536,768]{1,0:T(8,128)(2,1)})) %all-reduce.7.cloned.1.call-update) | async-done | bytes 4718608 | tf_op jit(solution)/shard_map/psum | solution.py:335
  270.5 3.0 convert_reduce_fusion
  273.7 3.4 psum.42
  277.0 76.0 %psum.43 = f32[6528]{0:T(1024)S(1)} all-reduce(f32[6528]{0:T(1024)S(1)} %pad_maximum_fusion.3), channel_id=1, replica_groups=mesh['dp'=16,'tensor'=2] {'dp'}, use_global_device_ids=true, to_apply=%region_16.17 | all-reduce | flops 6528 | bytes 52224 | tf_op jit(solution)/shard_map/psum | solution.py:375
  356.1 4.7 %convert_element_type.108 = f32[768,1536]{1,0:T(8,128)} convert(bf16[768,1536]{1,0:T(8,128)(2,1)} %get-tuple-element.31) | non-fusion elementwise | flops 1179648 | bytes 7077888 | tf_op jit(solution)/shard_map/convert_element_type | solution.py:395
  360.8 2.5 convert_element_type.109
  363.4 3.0 convert_reduce_fusion.2
  366.5 3.8 add_convert_fusion.3
  370.3 3.4 fusion.6
  373.7 63.6 %all-reduce.5.cloned.1.call-done = (bf16[3,768,384]{1,2,0:T(8,128)(2,1)}, bf16[384,768]{1,0:T(8,128)(2,1)}) async-done(((bf16[3,768,384]{1,2,0:T(8,128)(2,1)}, bf16[384,768]{1,0:T(8,128)(2,1)}), (bf16[3,768,384]{1,2,0:T(8,128)(2,1)}, bf16[384,768]{1,0:T(8,128)(2,1)})) %all-reduce.5.cloned.1.call-update) | async-done | bytes 2359312 | tf_op jit(solution)/shard_map/psum | solution.py:375
  437.3 2.2 convert_element_type.107
  439.5 4.0 copy.50
  (94 shorter events, 9.1 us)
Async XLA Ops:
  7.2 87.9 %copy-start = (bf16[3,768,384]{2,1,0:T(8,128)(2,1)S(1)}, bf16[3,768,384]{2,1,0:T(8,128)(2,1)}, u32[]{:S(2)}) copy-start(bf16[3,768,384]{2,1,0:T(8,128)(2,1)} %param.17) | copy-start | bytes 5308420
  7.2 6.8 %copy-start.13 = (bf16[2,768]{1,0:T(2,128)(2,1)S(1)}, bf16[2,768]{1,0:T(2,128)(2,1)}, u32[]{:S(2)}) copy-start(bf16[2,768]{1,0:T(2,128)(2,1)} %param.15) | copy-start | bytes 9220
  7.2 6.9 %copy-start.14 = (bf16[2,768]{1,0:T(2,128)(2,1)S(1)}, bf16[2,768]{1,0:T(2,128)(2,1)}, u32[]{:S(2)}) copy-start(bf16[2,768]{1,0:T(2,128)(2,1)} %param.16) | copy-start | bytes 9220
  7.2 6.9 %copy-start.12 = (bf16[1536]{0:T(1024)(128)(2,1)S(1)}, bf16[1536]{0:T(1024)(128)(2,1)}, u32[]{:S(2)}) copy-start(bf16[1536]{0:T(1024)(128)(2,1)} %param.22) | copy-start | bytes 9220
  7.2 17.7 %all-gather.3.cloned.1.call-start = ((), (), s32[]{:S(2)}) async-start(), calls=%async_computation.2 | async-start | bytes 4718592 | tf_op jit(solution)/shard_map/all_gather | solution.py:325
  8.0 32.0 %all-gather.5.cloned.1.call-start = ((), (), s32[]{:S(2)}) async-start(), calls=%async_computation.3 | async-start | bytes 4718592 | tf_op jit(solution)/shard_map/all_gather | solution.py:327
  14.0 256.4 %all-reduce.7.cloned.1.call-start = ((), (), s32[]{:S(2)}) async-start(), calls=%async_computation.7 | async-start | bytes 9437184 | tf_op jit(solution)/shard_map/psum | solution.py:335
  19.2 5.0 %copy-start.6 = (s32[2048,1]{1,0:T(8,128)S(1)}, s32[2048,1]{1,0:T(8,128)}, u32[]{:S(2)}) copy-start(s32[2048,1]{1,0:T(8,128)} %copy.44) | copy-start | bytes 24580
  24.9 2.8 copy-start.1
  28.9 241.6 %copy-start.10 = (f32[2048]{0:T(1024)}, f32[2048]{0:T(1024)S(1)}, u32[]{:S(2)}) copy-start(f32[2048]{0:T(1024)S(1)} %add_rsqrt_fusion) | copy-start | bytes 24580
  89.0 0.7 copy-start.15
  89.0 1.1 copy-start.9
  89.0 274.3 %reduce-scatter.5.cloned.1.call-start = ((), (), s32[]{:S(2)}) async-start(), calls=%async_computation.5 | async-start | bytes 4718592 | tf_op jit(solution)/shard_map/reduce_scatter | solution.py:358
  90.1 5.0 %copy-start.2 = (bf16[2048,768]{1,0:T(8,128)(2,1)S(1)}, bf16[2048,768]{1,0:T(8,128)(2,1)}, u32[]{:S(2)}) copy-start(bf16[2048,768]{1,0:T(8,128)(2,1)} %all-gather.3.cloned.1.call-done) | copy-start | bytes 9437188
  190.9 1.4 copy-start.8
  190.9 175.6 %reduce-scatter.3.cloned.1.call-start = ((), (), s32[]{:S(2)}) async-start(), calls=%async_computation.4 | async-start | bytes 4718592 | tf_op jit(solution)/shard_map/reduce_scatter | solution.py:348
  198.8 238.5 %all-reduce.5.cloned.1.call-start = ((), (), s32[]{:S(2)}) async-start(), calls=%async_computation.6 | async-start | bytes 4718592 | tf_op jit(solution)/shard_map/psum | solution.py:375
  199.0 4.3 copy-start.3
  203.3 67.1 %copy-start.16 = (bf16[2,768]{1,0:T(2,128)(2,1)S(1)}, bf16[2,768]{1,0:T(2,128)(2,1)}, u32[]{:S(2)}) copy-start(bf16[2,768]{1,0:T(2,128)(2,1)} %param.20) | copy-start | bytes 9220
  270.4 3.2 copy-start.11
  356.1 4.7 %copy-start.7 = (bf16[1536,768]{1,0:T(8,128)(2,1)S(1)}, bf16[1536,768]{1,0:T(8,128)(2,1)}, u32[]{:S(2)}) copy-start(bf16[1536,768]{1,0:T(8,128)(2,1)} %get-tuple-element.32) | copy-start | bytes 7077892
  366.4 3.9 copy-start.4
  366.4 3.9 dynamic-slice-start
  366.5 3.8 copy-start.5
Sparse Core Ops, SparseCore 0:
  9.6 14.8 all-gather.2
  26.6 13.3 all-gather.4
  89.2 181.1 all-reduce.6
  272.6 9.8 reduce-scatter.4
  285.2 12.0 reduce-scatter.2
  304.3 132.9 all-reduce.4
